TPU v7x, 256 devices: a whole 4x4x8 slice. The times are simulated.
256 devices in a mesh: lat: 128 (over x, z, y), lev: 2 (over core).
Axes of the slice: x: 4, y: 4, z: 8, core: 2. Of those that a mesh axis runs over, the one named last changes fastest.
Arguments:
- grid: bfloat16 [768, 2, 48, 3088], P('lat', None, 'lev'), may hold values from -6 to 6
- point_counts: int32 [768], P('lat'), may hold values from 16 to 3088, as said below
- waves: int32 [768], replicated, may hold values from 0 to 767, each once
- legendre: bfloat16 [768, 768, 768], P('lat'), may hold values from -0.21875 to 0.21875
- weights: float32 [768], P('lat'), may hold values from 0.5 to 2
- stiffness: float32 [48], replicated, may hold values from 1e-06 to 0.0001
Outputs:
- grid_out: bfloat16 [768, 2, 48, 3088], P('lat', None, 'lev')
Inputs may be any that keep to these rules, and one draw needn't show every extreme that they name: point_counts[j] is 4 j + 16 or 4 j + 20 (j counted from 0 at the pole), and the last pair has exactly 3088 points. `waves`: each wavenumber from 0 to 767 appears once.
All inputs are finite; a program needn't handle non-finite values.
Results may differ from a plain program's by a relative error of at most 0.015.
Values may be sent and summed in bfloat16 or wider, within the bound.
A program may use at most 128 MiB of HBM per device.

v0:
```python
import math

import jax
import jax.numpy as jnp
from jax import lax
from jax.sharding import PartitionSpec as P

TWO_PI = 2.0 * math.pi
FINE_STEPS = 32


def fourier_tables(count, wavenumbers, quarter_max):
    quarter = count // 4
    step_angle = TWO_PI / quarter.astype(jnp.float32)
    coarse_count = (quarter_max + FINE_STEPS - 1) // FINE_STEPS
    coarse_pos = FINE_STEPS * jnp.arange(coarse_count, dtype=jnp.int32)
    fine_pos = jnp.arange(FINE_STEPS, dtype=jnp.int32)
    coarse_angle = (coarse_pos[:, None] * wavenumbers[None, :] % quarter).astype(
        jnp.float32
    ) * step_angle
    fine_angle = (fine_pos[:, None] * wavenumbers[None, :] % quarter).astype(
        jnp.float32
    ) * step_angle
    coarse_cos = jnp.cos(coarse_angle)[:, None, :]
    coarse_sin = jnp.sin(coarse_angle)[:, None, :]
    fine_cos = jnp.cos(fine_angle)[None, :, :]
    fine_sin = jnp.sin(fine_angle)[None, :, :]
    full_cos = (coarse_cos * fine_cos - coarse_sin * fine_sin).reshape(
        coarse_count * FINE_STEPS, -1
    )[:quarter_max]
    full_sin = (coarse_sin * fine_cos + coarse_cos * fine_sin).reshape(
        coarse_count * FINE_STEPS, -1
    )[:quarter_max]
    positions = jnp.arange(quarter_max, dtype=jnp.int32)
    inside = (positions < quarter)[:, None]
    cosine = jnp.where(inside, full_cos, 0.0)
    sine = jnp.where(inside, full_sin, 0.0)
    matrix = jnp.concatenate([cosine, sine], axis=1).astype(jnp.bfloat16)
    offsets = jnp.arange(4, dtype=jnp.int32)
    twist = offsets[:, None] * wavenumbers[None, :] % count
    theta = twist.astype(jnp.float32) * (TWO_PI / count.astype(jnp.float32))
    return (matrix, jnp.cos(theta), jnp.sin(theta))


def helmholtz(spectra, wavenumbers, offsets, stiffness_local, width):
    full_shape = spectra.shape
    quartered = spectra.reshape(full_shape[:-2] + (full_shape[-2] // 4, 2, 2, full_shape[-1]))
    parity = (1 - 2 * (offsets % 2)).astype(jnp.float32)
    combined = quartered[..., 0, :] + parity * quartered[..., 1, :]
    degrees = (wavenumbers + offsets).astype(jnp.float32)
    inside_band = offsets < width - wavenumbers
    factor = 1.0 / (
        1.0 + stiffness_local[:, None] * degrees[..., None, :] * (degrees[..., None, :] + 1.0)
    )
    damping = jnp.where(inside_band[..., None, :], factor, 0.0)
    scaled = (combined * damping[..., :, None, :]).astype(jnp.bfloat16)
    flipped = scaled * parity.astype(jnp.bfloat16)
    return jnp.stack([scaled, flipped], axis=-2).reshape(full_shape)


def spectral(received, wavenumbers, basis, stiffness_local):
    width = basis.shape[2]
    spectra = jnp.einsum("jcr,cjl->crl", received, basis, preferred_element_type=jnp.float32)
    offsets = jnp.arange(width, dtype=jnp.int32)
    operand = helmholtz(spectra, wavenumbers[:, None], offsets, stiffness_local, width)
    returned = jnp.einsum("crl,cjl->jcr", operand, basis, preferred_element_type=jnp.float32)
    return returned.astype(jnp.bfloat16)


def on_device(grid, point_counts, waves, legendre, weights, stiffness):
    pairs, _, fields, points = grid.shape
    quarter_max = points // 4
    width = waves.shape[0]
    held_slots = legendre.shape[0]
    lat_index = lax.axis_index("lat")
    lev_index = lax.axis_index("lev")

    def analyse(pieces):
        latitude, count, weight = pieces
        matrix, twist_cos, twist_sin = fourier_tables(count, waves, quarter_max)
        values = latitude.reshape(2, fields, quarter_max, 4)
        partial_value = jnp.einsum(
            "hfab,at->hfbt", values, matrix, preferred_element_type=jnp.float32
        )
        cos_part = partial_value[..., :width]
        sin_part = partial_value[..., width:]
        real = jnp.sum(twist_cos * cos_part - twist_sin * sin_part, axis=2)
        imag = -jnp.sum(twist_sin * cos_part + twist_cos * sin_part, axis=2)
        factor = jnp.where(2 * waves < count, weight / count.astype(jnp.float32), 0.0)
        stacked = jnp.stack([real * factor, imag * factor], axis=0)
        packed = jnp.transpose(stacked, (3, 2, 0, 1)).reshape(width, 4 * fields)
        return (packed.astype(jnp.bfloat16), matrix, twist_cos, twist_sin)

    coefficients, matrices, twist_cos, twist_sin = lax.map(analyse, (grid, point_counts, weights))
    received = lax.all_to_all(coefficients, "lat", split_axis=1, concat_axis=0, tiled=True)
    owned = lax.dynamic_slice_in_dim(waves, lat_index * held_slots, held_slots)
    own_stiffness = lax.dynamic_slice_in_dim(stiffness, lev_index * fields, fields)
    synthesised = spectral(received, owned, legendre, own_stiffness)
    returned = lax.all_to_all(synthesised, "lat", split_axis=0, concat_axis=1, tiled=True)

    def synthesise(pieces):
        packed, matrix, turn_cos, turn_sin, count = pieces
        values = packed.astype(jnp.float32).reshape(width, fields, 2, 2)
        real = values[:, :, 0, :]
        imag = values[:, :, 1, :]
        factor = jnp.where(2 * waves < count, jnp.where(waves == 0, 1.0, 2.0), 0.0)[:, None, None]
        cosines = turn_cos[:, :, None, None]
        sines = turn_sin[:, :, None, None]
        turned_real = factor * (real * cosines - imag * sines)
        turned_imag = factor * (real * sines + imag * cosines)
        operand = jnp.concatenate([turned_real, -turned_imag], axis=1)
        upper = operand.astype(jnp.bfloat16)
        lower = (operand - upper.astype(jnp.float32)).astype(jnp.bfloat16)
        result = jnp.einsum("bmfh,am->hfab", upper, matrix, preferred_element_type=jnp.float32)
        result = result + jnp.einsum(
            "bmfh,am->hfab", lower, matrix, preferred_element_type=jnp.float32
        )
        return result.reshape(2, fields, points).astype(jnp.bfloat16)

    return lax.map(synthesise, (returned, matrices, twist_cos, twist_sin, point_counts))


def solution(mesh):
    in_specs = (P("lat", None, "lev", None), P("lat"), P(), P("lat", None, None), P("lat"), P())
    out_specs = P("lat", None, "lev", None)
    return jax.shard_map(
        on_device, mesh=mesh, in_specs=in_specs, out_specs=out_specs, check_vma=False
    )
```

profile of v0, /device:TPU:6, one launch (start us, length us, event | category | flops | bytes accessed | tf_op | source)
XLA Modules:
  0.0 338.8 jit_solution(2678139016416206473)
XLA Ops:
  0.0 142.9 %while.28 = (s32[]{:T(128)}, bf16[6,768,96]{1,2,0:T(8,128)(2,1)}, bf16[6,772,1536]{2,1,0:T(8,128)(2,1)}, f32[6,4,768]{2,1,0:T(4,128)}, f32[6,4,768]{2,1,0:T(4,12...) while((s32[]{:T(128)}, bf16[6,768,96]{1,2,0:T(8,128)(2,1)}, ...), condition=%wide.region_3.4_spmd, body=%wide.region_0.3_spmd.sunk | while | flops 472797760 | bytes 20898120 | solution.py:94
  3.6 2.1 fusion.90
  5.7 2.0 fusion.89
  13.1 3.4 %fusion.92 = f32[2,24,4,1536]{3,1,2,0:T(8,128)} fusion(bf16[772,768]{1,0:T(8,128)(2,1)S(1)} %get-tuple-element.389, bf16[772,768]{1,0:T(8,128)(2,1)S(1)} %get-tuple-element.390, bf16[2,24,772,4]{1,3,2,0:T(4,128)(2,1)} %bitcast.105), kind=kOutput, calls=%fused_computation.7.clone.1 | convolution fusion | flops 460087296 | bytes 3847680 | tf_op jit(solution)/shard_map/while/body/eval_jaxpr/hfab,at->hfbt/dot_general | solution.py:82
  27.4 2.1 fusion.90
  29.5 2.0 fusion.89
  36.9 3.4 %fusion.92 = f32[2,24,4,1536]{3,1,2,0:T(8,128)} fusion(bf16[772,768]{1,0:T(8,128)(2,1)S(1)} %get-tuple-element.389, bf16[772,768]{1,0:T(8,128)(2,1)S(1)} %get-tuple-element.390, bf16[2,24,772,4]{1,3,2,0:T(4,128)(2,1)} %bitcast.105), kind=kOutput, calls=%fused_computation.7.clone.1 | convolution fusion | flops 460087296 | bytes 3847680 | tf_op jit(solution)/shard_map/while/body/eval_jaxpr/hfab,at->hfbt/dot_general | solution.py:82
  51.2 2.1 fusion.90
  53.3 2.0 fusion.89
  60.8 3.4 %fusion.92 = f32[2,24,4,1536]{3,1,2,0:T(8,128)} fusion(bf16[772,768]{1,0:T(8,128)(2,1)S(1)} %get-tuple-element.389, bf16[772,768]{1,0:T(8,128)(2,1)S(1)} %get-tuple-element.390, bf16[2,24,772,4]{1,3,2,0:T(4,128)(2,1)} %bitcast.105), kind=kOutput, calls=%fused_computation.7.clone.1 | convolution fusion | flops 460087296 | bytes 3847680 | tf_op jit(solution)/shard_map/while/body/eval_jaxpr/hfab,at->hfbt/dot_general | solution.py:82
  75.0 2.1 fusion.90
  77.1 2.0 fusion.89
  84.6 3.4 %fusion.92 = f32[2,24,4,1536]{3,1,2,0:T(8,128)} fusion(bf16[772,768]{1,0:T(8,128)(2,1)S(1)} %get-tuple-element.389, bf16[772,768]{1,0:T(8,128)(2,1)S(1)} %get-tuple-element.390, bf16[2,24,772,4]{1,3,2,0:T(4,128)(2,1)} %bitcast.105), kind=kOutput, calls=%fused_computation.7.clone.1 | convolution fusion | flops 460087296 | bytes 3847680 | tf_op jit(solution)/shard_map/while/body/eval_jaxpr/hfab,at->hfbt/dot_general | solution.py:82
  98.9 2.1 fusion.90
  101.0 2.0 fusion.89
  108.4 3.4 %fusion.92 = f32[2,24,4,1536]{3,1,2,0:T(8,128)} fusion(bf16[772,768]{1,0:T(8,128)(2,1)S(1)} %get-tuple-element.389, bf16[772,768]{1,0:T(8,128)(2,1)S(1)} %get-tuple-element.390, bf16[2,24,772,4]{1,3,2,0:T(4,128)(2,1)} %bitcast.105), kind=kOutput, calls=%fused_computation.7.clone.1 | convolution fusion | flops 460087296 | bytes 3847680 | tf_op jit(solution)/shard_map/while/body/eval_jaxpr/hfab,at->hfbt/dot_general | solution.py:82
  122.7 2.1 fusion.90
  124.8 2.0 fusion.89
  132.2 3.4 %fusion.92 = f32[2,24,4,1536]{3,1,2,0:T(8,128)} fusion(bf16[772,768]{1,0:T(8,128)(2,1)S(1)} %get-tuple-element.389, bf16[772,768]{1,0:T(8,128)(2,1)S(1)} %get-tuple-element.390, bf16[2,24,772,4]{1,3,2,0:T(4,128)(2,1)} %bitcast.105), kind=kOutput, calls=%fused_computation.7.clone.1 | convolution fusion | flops 460087296 | bytes 3847680 | tf_op jit(solution)/shard_map/while/body/eval_jaxpr/hfab,at->hfbt/dot_general | solution.py:82
  142.9 2.8 copy.29
  145.7 16.1 %all-to-all-start = ((bf16[6,768,96]{2,0,1:T(8,128)(2,1)}), bf16[6,768,96]{2,0,1:T(8,128)(2,1)S(1)}, u32[]{:S(2)}, u32[]{:S(2)}) async-start(bf16[6,768,96]{2,0,1:T(8,128)(2,1)} %copy.29), calls=%async_computation | async-start | bytes 3145728 | tf_op jit(solution)/shard_map/all_to_all | solution.py:95
  163.2 38.2 %all-to-all-done = bf16[6,768,96]{2,0,1:T(8,128)(2,1)S(1)} async-done(((bf16[6,768,96]{2,0,1:T(8,128)(2,1)}), bf16[6,768,96]{2,0,1:T(8,128)(2,1)S(1)}, u32[]{:S(2)}, u32[]{:S(2)}) %all-to-all-start) | async-done | bytes 884768 | tf_op jit(solution)/shard_map/all_to_all | solution.py:95
  202.3 4.3 %fusion.70 = f32[6,96,768]{2,1,0:T(8,128)S(1)} fusion(bf16[768,6,96]{2,0,1:T(8,128)(2,1)S(1)} %all_to_all.29, bf16[6,768,768]{2,1,0:T(8,128)(2,1)} %param.13), kind=kOutput, calls=%fused_computation.113 | convolution fusion | flops 679477248 | bytes 9732096 | tf_op jit(solution)/shard_map/jcr,cjl->crl/dot_general | solution.py:63
  207.6 2.9 broadcast_multiply_fusion
  210.6 2.0 pad_maximum_fusion.1
  212.9 5.3 %fusion.61 = bf16[768,6,96]{0,2,1:T(8,128)(2,1)S(1)} fusion(bf16[6,96,768]{2,1,0:T(8,128)(2,1)S(1)} %reshape.472, bf16[6,768,768]{2,1,0:T(8,128)(2,1)} %param.13), kind=kOutput, calls=%fused_computation.93 | convolution fusion | flops 679919616 | bytes 8847360 | tf_op jit(solution)/shard_map/crl,cjl->jcr/dot_general | solution.py:66
  218.2 1.9 copy.33
  220.1 8.9 %all-to-all-start.1 = ((bf16[768,6,96]{2,1,0:T(8,128)(2,1)}), bf16[768,6,96]{2,1,0:T(8,128)(2,1)S(1)}, u32[]{:S(2)}, u32[]{:S(2)}) async-start(bf16[768,6,96]{2,1,0:T(8,128)(2,1)} %copy.33), calls=%async_computation.1 | async-start | bytes 3145728 | tf_op jit(solution)/shard_map/all_to_all | solution.py:99
  229.0 38.5 %all-to-all-done.1 = bf16[768,6,96]{2,1,0:T(8,128)(2,1)S(1)} async-done(((bf16[768,6,96]{2,1,0:T(8,128)(2,1)}), bf16[768,6,96]{2,1,0:T(8,128)(2,1)S(1)}, u32[]{:S(2)}, u32[]{:S(2)}) %all-to-all-start.1) | async-done | bytes 884768 | tf_op jit(solution)/shard_map/all_to_all | solution.py:99
  269.0 69.8 %while.29 = (s32[]{:T(128)}, bf16[6,2,24,3088]{3,2,1,0:T(8,128)(2,1)}, bf16[6,772,1536]{2,1,0:T(8,128)(2,1)}, s32[768]{0:T(1024)S(1)}, s32[6]{0:T(128)S(1)}, /*i...) while((s32[]{:T(128)}, ...), condition=%wide.region_5.6_spmd, body=%wide.region_4.5_spmd.sunk | while | flops 915043584 | bytes 14169717 | solution.py:120
  271.6 2.8 fusion.99
  274.4 2.8 fusion.100
  277.2 2.0 copy.62
  283.2 2.8 fusion.99
  286.0 2.8 fusion.100
  288.8 2.0 copy.62
  294.9 2.8 fusion.99
  297.6 2.8 fusion.100
  300.4 2.0 copy.62
  306.5 2.8 fusion.99
  309.3 2.8 fusion.100
  312.1 2.0 copy.62
  318.1 2.8 fusion.99
  320.9 2.8 fusion.100
  323.7 2.0 copy.62
  329.7 2.8 fusion.99
  332.5 2.8 fusion.100
  335.3 2.0 copy.62
  (223 shorter events, 97.9 us)
Async XLA Ops:
  13.1 5.1 %copy-start = (s32[768]{0:T(1024)S(1)}, s32[768]{0:T(1024)}, u32[]{:S(2)}) copy-start(s32[768]{0:T(1024)} %get-tuple-element.448) | copy-start | bytes 9220 | tf_op jit(solution)/shard_map/while
  13.1 7.0 %copy-start.2 = (f32[6]{0:T(128)S(1)}, f32[6]{0:T(128)}, u32[]{:S(2)}) copy-start(f32[6]{0:T(128)} %get-tuple-element.451) | copy-start | bytes 76 | tf_op jit(solution)/shard_map/while
  36.9 5.1 %copy-start = (s32[768]{0:T(1024)S(1)}, s32[768]{0:T(1024)}, u32[]{:S(2)}) copy-start(s32[768]{0:T(1024)} %get-tuple-element.448) | copy-start | bytes 9220 | tf_op jit(solution)/shard_map/while
  36.9 7.0 %copy-start.2 = (f32[6]{0:T(128)S(1)}, f32[6]{0:T(128)}, u32[]{:S(2)}) copy-start(f32[6]{0:T(128)} %get-tuple-element.451) | copy-start | bytes 76 | tf_op jit(solution)/shard_map/while
  60.8 5.1 %copy-start = (s32[768]{0:T(1024)S(1)}, s32[768]{0:T(1024)}, u32[]{:S(2)}) copy-start(s32[768]{0:T(1024)} %get-tuple-element.448) | copy-start | bytes 9220 | tf_op jit(solution)/shard_map/while
  60.8 7.0 %copy-start.2 = (f32[6]{0:T(128)S(1)}, f32[6]{0:T(128)}, u32[]{:S(2)}) copy-start(f32[6]{0:T(128)} %get-tuple-element.451) | copy-start | bytes 76 | tf_op jit(solution)/shard_map/while
  84.6 5.1 %copy-start = (s32[768]{0:T(1024)S(1)}, s32[768]{0:T(1024)}, u32[]{:S(2)}) copy-start(s32[768]{0:T(1024)} %get-tuple-element.448) | copy-start | bytes 9220 | tf_op jit(solution)/shard_map/while
  84.6 7.0 %copy-start.2 = (f32[6]{0:T(128)S(1)}, f32[6]{0:T(128)}, u32[]{:S(2)}) copy-start(f32[6]{0:T(128)} %get-tuple-element.451) | copy-start | bytes 76 | tf_op jit(solution)/shard_map/while
  108.4 5.1 %copy-start = (s32[768]{0:T(1024)S(1)}, s32[768]{0:T(1024)}, u32[]{:S(2)}) copy-start(s32[768]{0:T(1024)} %get-tuple-element.448) | copy-start | bytes 9220 | tf_op jit(solution)/shard_map/while
  108.4 7.0 %copy-start.2 = (f32[6]{0:T(128)S(1)}, f32[6]{0:T(128)}, u32[]{:S(2)}) copy-start(f32[6]{0:T(128)} %get-tuple-element.451) | copy-start | bytes 76 | tf_op jit(solution)/shard_map/while
  132.2 5.1 %copy-start = (s32[768]{0:T(1024)S(1)}, s32[768]{0:T(1024)}, u32[]{:S(2)}) copy-start(s32[768]{0:T(1024)} %get-tuple-element.448) | copy-start | bytes 9220 | tf_op jit(solution)/shard_map/while
  132.2 7.0 %copy-start.2 = (f32[6]{0:T(128)S(1)}, f32[6]{0:T(128)}, u32[]{:S(2)}) copy-start(f32[6]{0:T(128)} %get-tuple-element.451) | copy-start | bytes 76 | tf_op jit(solution)/shard_map/while
  145.7 16.1 %copy-start.3 = (f32[48]{0:T(128)S(1)}, f32[48]{0:T(128)}, u32[]{:S(2)}) copy-start(f32[48]{0:T(128)} %param.15) | copy-start | bytes 580
  145.7 16.2 %copy-start.1 = (s32[768]{0:T(1024)S(1)}, s32[768]{0:T(1024)}, u32[]{:S(2)}) copy-start(s32[768]{0:T(1024)} %get-tuple-element.487) | copy-start | bytes 9220
  145.7 55.6 %all-to-all-start = ((bf16[6,768,96]{2,0,1:T(8,128)(2,1)}), bf16[6,768,96]{2,0,1:T(8,128)(2,1)S(1)}, u32[]{:S(2)}, u32[]{:S(2)}) async-start(bf16[6,768,96]{2,0,1:T(8,128)(2,1)} %copy.29), calls=%async_computation | async-start | bytes 3145728 | tf_op jit(solution)/shard_map/all_to_all | solution.py:95
  220.1 47.4 %all-to-all-start.1 = ((bf16[768,6,96]{2,1,0:T(8,128)(2,1)}), bf16[768,6,96]{2,1,0:T(8,128)(2,1)S(1)}, u32[]{:S(2)}, u32[]{:S(2)}) async-start(bf16[768,6,96]{2,1,0:T(8,128)(2,1)} %copy.33), calls=%async_computation.1 | async-start | bytes 3145728 | tf_op jit(solution)/shard_map/all_to_all | solution.py:99
  267.7 1.3 copy-start.4
where the time goes:
time: 343 us; the launch traced here: 339 us
  waiting for transfers between devices  76.6 us (22%)
  other arithmetic  74.2 us (22%)
  local copies, waits for them, and re-layouts  70.3 us (20%)
  matrix products  63.4 us (18%)
  loops' own time  29.3 us (9%)
  starting transfers between devices  24.9 us (7%)
    all_to_all x1, waiting for transfers between devices, on_device(): lax.all_to_all(synthesised, 'lat', split_axis=0, concat_axis=1, tiled=True)  38.5 us
    all_to_all x1, waiting for transfers between devices, on_device(): lax.all_to_all(coefficients, 'lat', split_axis=1, concat_axis=0, tiled=True)  38.2 us
    dynamic_slice x30, local copies, waits for them, and re-layouts, on_device(): lax.map(analyse, (grid, point_counts, weights))  29.9 us
    another operation x1, loops' own time, on_device(): lax.map(analyse, (grid, point_counts, weights))  28.8 us
    dot_general x6, matrix products, analyse(): jnp.einsum('hfab,at->hfbt', values, matrix, preferred_element_type=jnp.fl...  20.4 us
    dot_general x6, matrix products, synthesise(): jnp.einsum('bmfh,am->hfab', upper, matrix, preferred_element_type=jnp.flo...  16.7 us
    dot_general x6, matrix products, synthesise(): jnp.einsum('bmfh,am->hfab', lower, matrix, preferred_element_type=jnp.flo...  16.6 us
    all_to_all x1, starting transfers between devices, on_device(): lax.all_to_all(coefficients, 'lat', split_axis=1, concat_axis=0, tiled=True)  16.1 us
  transfers between devices with their start and end apart: 2, of which 2 were waited for; matrix products, arithmetic and copies ran while one was open for 0% of the time, Pallas kernels for 0%

commit v1 on v0

v1 whole, which is shorter than its diff:
```python
import functools
import math

import jax
import jax.numpy as jnp
from jax import lax
from jax.experimental import pallas as pl
from jax.experimental.pallas import tpu as pltpu
from jax.sharding import PartitionSpec as P

MESH = pl.DeviceIdType.MESH
F32 = jnp.float32
BF16 = jnp.bfloat16
LANES = 128
BLOCK = 256
FINE = 16
NT = (((1,), (1,)), ((), ()))


def cos_sin(steps, waves, count, inverse):
    product = steps * waves
    turns = jnp.floor(product * inverse + 0.5)
    half = (product - turns * count) * inverse * math.pi
    square = half * half
    sine = half
    term = 1.0
    series_s, series_c = 0.0, 0.0
    for power in range(5, -1, -1):
        series_s = series_s * square + (-1.0) ** power / math.factorial(2 * power + 1)
    for power in range(6, -1, -1):
        series_c = series_c * square + (-1.0) ** power / math.factorial(2 * power)
    sine = half * series_s
    return 1.0 - 2.0 * sine * sine, 2.0 * sine * series_c


def kernel(
    shape,
    grid_ref, counts_ref, weights_ref, waves_smem, waves_ref, stiffness_ref, legendre_ref,
    out_ref,
    tables, turn_c, turn_s, small_c, small_s, points, flat, spread, basis, ordered, perm, damping,
    spectra, scaled, operand, turned,
    send_a, recv_a, send_b, recv_b, basis_sem, send_sems, recv_sems,
):
    holders, pairs, fields, length, slots, width = shape
    chunks = 2
    lats = pairs // chunks
    blocks = -(-length // BLOCK)
    rows = 2 * fields
    parts = 2 * rows
    per_lat = slots * parts
    held = lats * per_lat
    pieces = -(-held // LANES)
    deep = send_a.shape[2]
    me = lax.axis_index("lat")
    lev = lax.axis_index("lev")

    barrier = pltpu.get_barrier_semaphore()

    def greet(k, carry):
        other = lax.rem(me + k, holders)
        pl.semaphore_signal(barrier, inc=1, device_id=(other, lev), device_id_type=MESH)
        return carry

    lax.fori_loop(1, holders, greet, 0)
    load_basis = pltpu.make_async_copy(legendre_ref, basis, basis_sem)
    load_basis.start()

    spread[...] = jnp.zeros_like(spread)
    flat[pl.ds(held, pieces * LANES - held), :] = jnp.zeros((pieces * LANES - held, LANES), F32)
    points[...] = jnp.zeros_like(points)

    def build_tables(i):
        count = jnp.full((1, width), counts_ref[i].astype(F32), F32)
        inverse = 1.0 / count
        waves = waves_ref[...].astype(F32)
        steps = lax.broadcasted_iota(jnp.int32, (FINE, width), 0).astype(F32)
        fine_c, fine_s = cos_sin(steps, waves, count, inverse)
        coarse_c, coarse_s = cos_sin(steps * FINE, waves, count, inverse)
        block_c, block_s = cos_sin(steps * BLOCK, waves, count, inverse)
        small_c[...] = coarse_c
        small_s[...] = coarse_s
        turn_c[i] = block_c
        turn_s[i] = block_s
        for g in range(BLOCK // FINE):
            c = small_c[g : g + 1, :]
            s = small_s[g : g + 1, :]
            tables[i, g * FINE : (g + 1) * FINE, :width] = (fine_c * c - fine_s * s).astype(BF16)
            tables[i, g * FINE : (g + 1) * FINE, width:] = (fine_s * c + fine_c * s).astype(BF16)

    def analyse(i, local):
        build_tables(i)
        total = counts_ref[i]
        for t in range(blocks):
            size = min(BLOCK, length - t * BLOCK)
            at = lax.broadcasted_iota(jnp.int32, (rows, size), 1) + t * BLOCK
            values = grid_ref[i, :, :, t * BLOCK : t * BLOCK + size].astype(F32)
            values = jnp.where(at < total, values.reshape(rows, size), 0.0)
            points[t * rows : (t + 1) * rows, :size] = values.astype(BF16)
        limit = total.astype(F32)
        scale = jnp.full((1, BLOCK), weights_ref[i], F32) / jnp.full((1, BLOCK), limit, F32)
        for n in range(width // BLOCK):
            lanes = slice(n * BLOCK, (n + 1) * BLOCK)
            by_c = jnp.dot(points[...], tables[i, :, lanes], preferred_element_type=F32)
            by_s = jnp.dot(
                points[...],
                tables[i, :, width + n * BLOCK : width + (n + 1) * BLOCK],
                preferred_element_type=F32,
            )
            real = by_c[:rows]
            imag = by_s[:rows]
            for t in range(1, blocks):
                c = turn_c[i, t : t + 1, lanes]
                s = turn_s[i, t : t + 1, lanes]
                zc = by_c[t * rows : (t + 1) * rows]
                zs = by_s[t * rows : (t + 1) * rows]
                real = real + (c * zc - s * zs)
                imag = imag + (s * zc + c * zs)
            inside = 2 * waves_ref[:, lanes] < total
            factor = jnp.where(inside, scale, 0.0)
            real = real * factor
            imag = -imag * factor
            for k in range(BLOCK // LANES):
                slot = n * (BLOCK // LANES) + k
                cut = slice(k * LANES, (k + 1) * LANES)
                for h in range(2):
                    base = local * per_lat + slot * parts + h * rows
                    if not isinstance(base, int):
                        base = pl.multiple_of(base, 8)
                    flat[pl.ds(base, fields), :] = real[h * fields : (h + 1) * fields, cut]
                    flat[pl.ds(base + fields, fields), :] = imag[h * fields : (h + 1) * fields, cut]

    def pack(target, chunk):
        for q in range(pieces):
            piece = flat[q * LANES : (q + 1) * LANES, :]
            spread[pl.ds(q, holders, stride=deep), :] = piece.T
        target[chunk] = spread[...].reshape(holders, deep, LANES).astype(BF16)

    def unpack(source, chunk):
        spread[...] = source[chunk].astype(F32).reshape(holders * deep, LANES)
        for q in range(pieces):
            flat[q * LANES : (q + 1) * LANES, :] = spread[pl.ds(q, holders, stride=deep), :].T

    def send(source, target, chunk, sem):
        def one(k, carry):
            other = lax.rem(me + k, holders)
            pltpu.make_async_remote_copy(
                src_ref=source.at[chunk, other],
                dst_ref=target.at[chunk, me],
                send_sem=send_sems.at[sem],
                recv_sem=recv_sems.at[sem],
                device_id=(other, lev),
                device_id_type=MESH,
            ).start()
            return carry

        lax.fori_loop(1, holders, one, 0)
        target[chunk, me] = source[chunk, me]

    def finish(ref, chunk, sem):
        most = ref.at[chunk, pl.ds(0, holders - 1)]
        pltpu.make_async_copy(most, most, sem).wait()

    for chunk in range(chunks):
        def step(local, carry):
            analyse(chunk * lats + local, local)
            return carry

        lax.fori_loop(0, lats, step, 0)
        pack(send_a, chunk)
        if chunk == 0:
            pl.semaphore_wait(barrier, holders - 1)
        send(send_a, recv_a, chunk, chunk)

    for i in range(pairs):
        place = lax.broadcasted_iota(jnp.int32, (holders, width), 0) * pairs + i
        at = lax.broadcasted_iota(jnp.int32, (holders, width), 1)
        perm[i * holders : (i + 1) * holders, :] = jnp.where(at == place, 1.0, 0.0).astype(BF16)
    load_basis.wait()

    levels = lax.broadcasted_iota(jnp.int32, (fields, stiffness_ref.shape[1]), 0) + lev * fields
    column = lax.broadcasted_iota(jnp.int32, (fields, stiffness_ref.shape[1]), 1)
    stiffness = jnp.sum(jnp.where(levels == column, stiffness_ref[...], 0.0), axis=1, keepdims=True)
    offsets = lax.broadcasted_iota(jnp.int32, (1, width), 1)
    parity = (1 - 2 * lax.rem(offsets, 2)).astype(F32)

    def prepare(s, carry):
        for m in range(width // BLOCK):
            part = slice(m * BLOCK, (m + 1) * BLOCK)
            ordered[s, part, :] = jnp.dot(
                perm[part, :], basis[s], preferred_element_type=F32
            ).astype(BF16)
        wave = waves_smem[me * slots + s]
        degrees = (offsets + wave).astype(F32)
        factor = 1.0 / (1.0 + stiffness * degrees * (degrees + 1.0))
        damping[s] = jnp.where(offsets < width - wave, factor, 0.0)
        return carry

    lax.fori_loop(0, slots, prepare, 0)

    half = lats * holders
    for chunk in range(chunks):
        finish(recv_a, chunk, recv_sems.at[chunk])
        unpack(recv_a, chunk)

        def forward(s, carry):
            pieces_of = [
                flat[pl.ds(pl.multiple_of(i * per_lat + s * parts, 8), parts), :].astype(BF16)
                for i in range(lats)
            ]
            part = jnp.dot(
                jnp.concatenate(pieces_of, axis=1),
                ordered[s, chunk * half : (chunk + 1) * half, :],
                preferred_element_type=F32,
            )
            if chunk == 0:
                spectra[s] = part
            else:
                part = part + spectra[s]
                combined = part[:rows] + parity * part[rows:]
                damp = jnp.concatenate([damping[s], damping[s]], axis=0)
                north = combined * damp
                scaled[s, :rows, :] = north.astype(BF16)
                scaled[s, rows:, :] = (north * parity).astype(BF16)
            return carry

        lax.fori_loop(0, slots, forward, 0)

    for chunk in range(chunks):
        def backward(s, carry):
            part = lax.dot_general(
                scaled[s],
                ordered[s, chunk * half : (chunk + 1) * half, :],
                NT,
                preferred_element_type=F32,
            )
            for i in range(lats):
                flat[pl.ds(pl.multiple_of(i * per_lat + s * parts, 8), parts), :] = part[
                    :, i * holders : (i + 1) * holders
                ]
            return carry

        lax.fori_loop(0, slots, backward, 0)
        pack(send_b, chunk)
        send(send_b, recv_b, chunk, chunks + chunk)

    def synthesise(i, local):
        total = counts_ref[i]
        inside = 2 * waves_ref[...] < total
        weight = jnp.where(inside, jnp.where(waves_ref[...] == 0, 1.0, 2.0), 0.0)
        for s in range(slots):
            lanes = slice(s * LANES, (s + 1) * LANES)
            for h in range(2):
                base = pl.multiple_of(local * per_lat + s * parts + h * rows, 8)
                operand[0, h * fields : (h + 1) * fields, lanes] = (
                    flat[pl.ds(base, fields), :] * weight[:, lanes]
                )
                operand[1, h * fields : (h + 1) * fields, lanes] = (
                    flat[pl.ds(base + fields, fields), :] * weight[:, lanes]
                )
        for n in range(width // BLOCK):
            lanes = slice(n * BLOCK, (n + 1) * BLOCK)
            real = operand[0, :, lanes]
            imag = operand[1, :, lanes]
            for t in range(blocks):
                c = turn_c[i, t : t + 1, lanes]
                s = turn_s[i, t : t + 1, lanes]
                turned[t * rows : (t + 1) * rows, lanes] = (real * c - imag * s).astype(BF16)
                turned[t * rows : (t + 1) * rows, width + n * BLOCK : width + (n + 1) * BLOCK] = (
                    -(real * s + imag * c)
                ).astype(BF16)
        result = lax.dot_general(turned[...], tables[i], NT, preferred_element_type=F32)
        for t in range(blocks):
            size = min(BLOCK, length - t * BLOCK)
            at = lax.broadcasted_iota(jnp.int32, (rows, size), 1) + t * BLOCK
            values = jnp.where(at < total, result[t * rows : (t + 1) * rows, :size], 0.0)
            out_ref[i, :, :, t * BLOCK : t * BLOCK + size] = values.reshape(2, fields, size).astype(BF16)

    for chunk in range(chunks):
        finish(recv_b, chunk, recv_sems.at[chunks + chunk])
        unpack(recv_b, chunk)

        def step_back(local, carry):
            synthesise(chunk * lats + local, local)
            return carry

        lax.fori_loop(0, lats, step_back, 0)

    for chunk in range(chunks):
        finish(send_a, chunk, send_sems.at[chunk])
        finish(send_b, chunk, send_sems.at[chunks + chunk])


def solution(mesh):
    holders = mesh.shape["lat"]

    def on_device(grid, point_counts, waves, legendre, weights, stiffness):
        pairs, _, fields, length = grid.shape
        slots, latitudes, width = legendre.shape
        blocks = -(-length // BLOCK)
        rows = 2 * fields
        held = (pairs // 2) * slots * 2 * rows
        pieces = -(-held // LANES)
        deep = -(-pieces // 16) * 16
        by_slot = waves.reshape(holders, slots).T.reshape(1, width)
        smem = pl.BlockSpec(memory_space=pltpu.SMEM)
        vmem = pl.BlockSpec(memory_space=pltpu.VMEM)
        message = pltpu.VMEM((2, holders, deep, LANES), BF16)
        return pl.pallas_call(
            functools.partial(kernel, (holders, pairs, fields, length, slots, width)),
            out_shape=jax.ShapeDtypeStruct(grid.shape, grid.dtype),
            in_specs=[vmem, smem, smem, smem, vmem, vmem, pl.BlockSpec(memory_space=pl.ANY)],
            out_specs=vmem,
            scratch_shapes=[
                pltpu.VMEM((pairs, BLOCK, 2 * width), BF16),
                pltpu.VMEM((pairs, FINE, width), F32),
                pltpu.VMEM((pairs, FINE, width), F32),
                pltpu.VMEM((FINE, width), F32),
                pltpu.VMEM((FINE, width), F32),
                pltpu.VMEM((blocks * rows, BLOCK), BF16),
                pltpu.VMEM((pieces * LANES, LANES), F32),
                pltpu.VMEM((holders * deep, LANES), F32),
                pltpu.VMEM((slots, latitudes, width), BF16),
                pltpu.VMEM((slots, latitudes, width), BF16),
                pltpu.VMEM((latitudes, width), BF16),
                pltpu.VMEM((slots, fields, width), F32),
                pltpu.VMEM((slots, 2 * rows, width), F32),
                pltpu.VMEM((slots, 2 * rows, width), BF16),
                pltpu.VMEM((2, rows, width), F32),
                pltpu.VMEM((blocks * rows, 2 * width), BF16),
                message,
                message,
                message,
                message,
                pltpu.SemaphoreType.DMA,
                pltpu.SemaphoreType.DMA((4,)),
                pltpu.SemaphoreType.DMA((4,)),
            ],
            compiler_params=pltpu.CompilerParams(
                collective_id=0, has_side_effects=True, vmem_limit_bytes=56 * 2**20
            ),
        )(grid, point_counts, weights, waves, by_slot, stiffness.reshape(1, -1), legendre)

    in_specs = (P("lat", None, "lev", None), P("lat"), P(), P("lat", None, None), P("lat"), P())
    out_specs = P("lat", None, "lev", None)
    return jax.shard_map(
        on_device, mesh=mesh, in_specs=in_specs, out_specs=out_specs, check_vma=False
    )
```

time: 343 us -> 78 us (0.23); the launches traced: 339 us -> 77.9 us
  waiting for transfers between devices: 76.6 us -> 0 us
  other arithmetic: 74.2 us -> 0 us
  Pallas kernels: 0 us -> 73.5 us
  local copies, waits for them, and re-layouts: 70.3 us -> 4.34 us
  matrix products: 63.4 us -> 0 us
  loops' own time: 29.3 us -> 0 us
  starting transfers between devices: 24.9 us -> 0 us
    all_to_all x2 -> x0, waiting for transfers between devices: 76.6 us -> none  [the longest x1 38.5 us: on_device(): lax.all_to_all(synthesised, 'lat', split_axis=0, concat_axis=1, tiled=True)]
    pallas_call x0 -> x1, Pallas kernels: none -> 73.5 us  [on_device(): pl.pallas_call(functools.partial(kernel, (holders, pairs, fields, length,...]
    dot_general x20 -> x0, matrix products: 63.4 us -> none  [the longest x6 20.4 us: analyse(): jnp.einsum('hfab,at->hfbt', values, matrix, preferred_element_type=jnp.fl...]
    dynamic_slice x31 -> x0, local copies, waits for them, and re-layouts: 30 us -> none  [the longest x30 29.9 us: on_device(): lax.map(analyse, (grid, point_counts, weights))]
    another operation x2 -> x0, loops' own time: 29.3 us -> none  [the longest x1 28.8 us: on_device(): lax.map(analyse, (grid, point_counts, weights))]
    cos x18 -> x0, other arithmetic: 27.1 us -> none  [the longest x6 12.6 us: fourier_tables(): coarse_cos = jnp.cos(coarse_angle)[:, None, :]]
    all_to_all x2 -> x0, starting transfers between devices: 24.9 us -> none  [the longest x1 16.1 us: on_device(): lax.all_to_all(coefficients, 'lat', split_axis=1, concat_axis=0, tiled=True)]
    convert_element_type x25 -> x0, local copies, waits for them, and re-layouts: 16.2 us -> none  [the longest x6 12.2 us: synthesise(): return result.reshape(2, fields, points).astype(jnp.bfloat16)]
  transfers between devices with their start and end apart: 2 -> 0, of which waited for: 2 -> 0; matrix products, arithmetic and copies ran while one was open for 0% -> 0% of each run, Pallas kernels for 0% -> 0%
where the time goes in v1:
time: 78 us; the launch traced here: 77.9 us
  Pallas kernels  73.5 us (94%)
  local copies, waits for them, and re-layouts  4.34 us (6%)
    pallas_call x1, Pallas kernels, on_device(): pl.pallas_call(functools.partial(kernel, (holders, pairs, fields, length,...  73.5 us
    unnamed x2, local copies, waits for them, and re-layouts  3.47 us

profile of v1, /device:TPU:6, one launch (start us, length us, event | category | flops | bytes accessed | tf_op | source)
XLA Modules:
  0.0 77.9 jit_solution(17613014912885941771)
XLA Ops:
  0.0 0.8 %reshape.9 = s32[128,6]{1,0:T(8,128)S(1)} reshape(s32[768]{0:T(1024)} %waves_smem.1) | data formatting | bytes 6144 | tf_op jit(solution)/shard_map/reshape | solution.py:304
  0.8 0.1 copy.7
  0.9 0.6 copy.10
  1.5 73.5 %shard_map.64 = bf16[6,2,24,3088]{3,2,1,0:T(8,128)(2,1)} custom-call(bf16[6,2,24,3088]{3,2,1,0:T(8,128)(2,1)} %grid_ref.1, s32[6]{0:T(128)} %counts_ref.1, f32[6]{0:T(128)} %weights_ref.1, s32[768]{0:T(1024)} %waves_smem.1, s32[1,768]{1,0:T(1,128)} %bitcast.9, f32[1,48]{1,0:T(1,128)} %bitcast.10, bf16[6,768,768]{2,1,0:T(8,128)(2,1)} %legendre_ref.1), custom_call_target="tpu_custom_call" | custom-call | tf_op jit(solution)/shard_map/pallas_call | solution.py:308
  75.0 2.9 %copy.12 = bf16[6,2,24,3088]{3,2,1,0:T(8,128)(2,1)} copy(bf16[6,2,24,3088]{3,2,1,0:T(8,128)(2,1)} %shard_map.64) | data formatting | bytes 3557376

commit v2 on v1

--- a/solution.py
+++ b/solution.py
@@ -14,6 +14,7 @@
 LANES = 128
 BLOCK = 256
 FINE = 16
+VMEM_LIMIT = 60 * 2**20
 NT = (((1,), (1,)), ((), ()))
 
 
@@ -35,9 +36,9 @@
 
 def kernel(
     shape,
-    grid_ref, counts_ref, weights_ref, waves_smem, waves_ref, stiffness_ref, legendre_ref,
+    grid_ref, counts_ref, weights_ref, waves_smem, wave_row, stiffness_ref, legendre_ref,
     out_ref,
-    tables, turn_c, turn_s, small_c, small_s, points, flat, spread, basis, ordered, perm, damping,
+    waves_ref, tables, turn_c, turn_s, small_c, small_s, points, flat, spread, basis, ordered, perm, damping,
     spectra, scaled, operand, turned,
     send_a, recv_a, send_b, recv_b, basis_sem, send_sems, recv_sems,
 ):
@@ -50,7 +51,7 @@
     per_lat = slots * parts
     held = lats * per_lat
     pieces = -(-held // LANES)
-    deep = send_a.shape[2]
+    deep = 2 * send_a.shape[2]
     me = lax.axis_index("lat")
     lev = lax.axis_index("lev")
 
@@ -69,10 +70,22 @@
     flat[pl.ds(held, pieces * LANES - held), :] = jnp.zeros((pieces * LANES - held, LANES), F32)
     points[...] = jnp.zeros_like(points)
 
+    for i in range(pairs):
+        place = lax.broadcasted_iota(jnp.int32, (holders, width), 0) * pairs + i
+        at = lax.broadcasted_iota(jnp.int32, (holders, width), 1)
+        perm[i * holders : (i + 1) * holders, :] = jnp.where(at == place, 1.0, 0.0).astype(BF16)
+    order = wave_row[...].reshape(1, width)
+    first = lax.broadcasted_iota(jnp.int32, (16, width), 0) == 0
+    digits = jnp.where(first, order // LANES, lax.rem(order, LANES))
+    digits = lax.dot_general(
+        digits.astype(F32).astype(BF16), perm[...], NT, preferred_element_type=F32
+    )
+    waves_ref[...] = digits[:1] * LANES + digits[1:2]
+
     def build_tables(i):
         count = jnp.full((1, width), counts_ref[i].astype(F32), F32)
         inverse = 1.0 / count
-        waves = waves_ref[...].astype(F32)
+        waves = waves_ref[...]
         steps = lax.broadcasted_iota(jnp.int32, (FINE, width), 0).astype(F32)
         fine_c, fine_s = cos_sin(steps, waves, count, inverse)
         coarse_c, coarse_s = cos_sin(steps * FINE, waves, count, inverse)
@@ -115,7 +128,7 @@
                 zs = by_s[t * rows : (t + 1) * rows]
                 real = real + (c * zc - s * zs)
                 imag = imag + (s * zc + c * zs)
-            inside = 2 * waves_ref[:, lanes] < total
+            inside = 2.0 * waves_ref[:, lanes] < limit
             factor = jnp.where(inside, scale, 0.0)
             real = real * factor
             imag = -imag * factor
@@ -133,7 +146,8 @@
         for q in range(pieces):
             piece = flat[q * LANES : (q + 1) * LANES, :]
             spread[pl.ds(q, holders, stride=deep), :] = piece.T
-        target[chunk] = spread[...].reshape(holders, deep, LANES).astype(BF16)
+        pairs_of_rows = spread[...].reshape(holders * deep // 2, 2, LANES).astype(BF16)
+        target[chunk] = pairs_of_rows.reshape(holders, deep // 2, 2, LANES)
 
     def unpack(source, chunk):
         spread[...] = source[chunk].astype(F32).reshape(holders * deep, LANES)
@@ -171,10 +185,6 @@
             pl.semaphore_wait(barrier, holders - 1)
         send(send_a, recv_a, chunk, chunk)
 
-    for i in range(pairs):
-        place = lax.broadcasted_iota(jnp.int32, (holders, width), 0) * pairs + i
-        at = lax.broadcasted_iota(jnp.int32, (holders, width), 1)
-        perm[i * holders : (i + 1) * holders, :] = jnp.where(at == place, 1.0, 0.0).astype(BF16)
     load_basis.wait()
 
     levels = lax.broadcasted_iota(jnp.int32, (fields, stiffness_ref.shape[1]), 0) + lev * fields
@@ -245,7 +255,7 @@
 
     def synthesise(i, local):
         total = counts_ref[i]
-        inside = 2 * waves_ref[...] < total
+        inside = 2.0 * waves_ref[...] < total.astype(F32)
         weight = jnp.where(inside, jnp.where(waves_ref[...] == 0, 1.0, 2.0), 0.0)
         for s in range(slots):
             lanes = slice(s * LANES, (s + 1) * LANES)
@@ -290,6 +300,17 @@
         finish(send_b, chunk, send_sems.at[chunks + chunk])
 
 
+def write_out(source, target, sems):
+    copies = [
+        pltpu.make_async_copy(source.at[i], target.at[i], sems.at[i])
+        for i in range(source.shape[0])
+    ]
+    for copy in copies:
+        copy.start()
+    for copy in copies:
+        copy.wait()
+
+
 def solution(mesh):
     holders = mesh.shape["lat"]
 
@@ -300,17 +321,18 @@
         rows = 2 * fields
         held = (pairs // 2) * slots * 2 * rows
         pieces = -(-held // LANES)
-        deep = -(-pieces // 16) * 16
-        by_slot = waves.reshape(holders, slots).T.reshape(1, width)
+        deep = -(-pieces // 2) * 2
+        assert pairs == slots and holders * slots == width == latitudes
         smem = pl.BlockSpec(memory_space=pltpu.SMEM)
         vmem = pl.BlockSpec(memory_space=pltpu.VMEM)
-        message = pltpu.VMEM((2, holders, deep, LANES), BF16)
-        return pl.pallas_call(
+        message = pltpu.VMEM((2, holders, deep // 2, 2, LANES), BF16)
+        result = pl.pallas_call(
             functools.partial(kernel, (holders, pairs, fields, length, slots, width)),
-            out_shape=jax.ShapeDtypeStruct(grid.shape, grid.dtype),
+            out_shape=pltpu.VMEM(grid.shape, grid.dtype),
             in_specs=[vmem, smem, smem, smem, vmem, vmem, pl.BlockSpec(memory_space=pl.ANY)],
             out_specs=vmem,
             scratch_shapes=[
+                pltpu.VMEM((1, width), F32),
                 pltpu.VMEM((pairs, BLOCK, 2 * width), BF16),
                 pltpu.VMEM((pairs, FINE, width), F32),
                 pltpu.VMEM((pairs, FINE, width), F32),
@@ -336,9 +358,17 @@
                 pltpu.SemaphoreType.DMA((4,)),
             ],
             compiler_params=pltpu.CompilerParams(
-                collective_id=0, has_side_effects=True, vmem_limit_bytes=56 * 2**20
+                collective_id=0, has_side_effects=True, vmem_limit_bytes=VMEM_LIMIT
             ),
-        )(grid, point_counts, weights, waves, by_slot, stiffness.reshape(1, -1), legendre)
+        )(grid, point_counts, weights, waves, waves, stiffness.reshape(1, -1), legendre)
+        anywhere = pl.BlockSpec(memory_space=pl.ANY)
+        return pl.pallas_call(
+            write_out,
+            out_shape=jax.ShapeDtypeStruct(grid.shape, grid.dtype),
+            in_specs=[vmem],
+            out_specs=anywhere,
+            scratch_shapes=[pltpu.SemaphoreType.DMA((pairs,))],
+        )(pltpu.with_memory_space_constraint(result, pltpu.VMEM))
 
     in_specs = (P("lat", None, "lev", None), P("lat"), P(), P("lat", None, None), P("lat"), P())
     out_specs = P("lat", None, "lev", None)

time: 78 us -> 68.7 us (0.88)
  Pallas kernels: 73.5 us -> 68.5 us
  local copies, waits for them, and re-layouts: 4.34 us -> 0 us
    pallas_call x1, Pallas kernels: 73.5 us -> 67.3 us  [on_device(): pl.pallas_call(functools.partial(kernel, (holders, pairs, fields, length,...]
    unnamed x2 -> x0, local copies, waits for them, and re-layouts: 3.47 us -> none
    pallas_call x0 -> x1, Pallas kernels: none -> 1.28 us  [on_device(): pl.pallas_call(write_out, out_shape=jax.ShapeDtypeStruct(grid.shape, grid...]
    reshape x1 -> x0, local copies, waits for them, and re-layouts: 0.81 us -> none  [on_device(): by_slot = waves.reshape(holders, slots).T.reshape(1, width)]
where the time goes in v2:
time: 68.7 us; the launch traced here: 68.6 us
  Pallas kernels  68.5 us (100%)
    pallas_call x1, Pallas kernels, on_device(): pl.pallas_call(functools.partial(kernel, (holders, pairs, fields, length,...  67.3 us

profile of v2, /device:TPU:6, one launch (start us, length us, event | category | flops | bytes accessed | tf_op | source)
XLA Modules:
  0.0 68.6 jit_solution(18292873450094147497)
XLA Ops:
  0.0 67.3 %shard_map.64.source = bf16[6,2,24,3088]{3,2,1,0:T(8,128)(2,1)S(1)} custom-call(bf16[6,2,24,3088]{3,2,1,0:T(8,128)(2,1)} %grid_ref.1, s32[6]{0:T(128)} %counts_ref.1, f32[6]{0:T(128)} %weights_ref.1, s32[768]{0:T(1024)} %wave_row.1, s32[768]{0:T(1024)} %wave_row.1, f32[1,48]{1,0:T(1,128)} %bitcast.1, bf16[6,768,768]{2,1,0:T(8,128)(2,1)} %legendre_ref.1), custom_call_target="tpu_custom_call" | custom-call | tf_op jit(solution)/shard_map/pallas_call | solution.py:329
  67.3 1.3 %shard_map.65 = bf16[6,2,24,3088]{3,2,1,0:T(8,128)(2,1)} custom-call(bf16[6,2,24,3088]{3,2,1,0:T(8,128)(2,1)S(1)} %shard_map.64.source), custom_call_target="tpu_custom_call" | custom-call | tf_op jit(solution)/shard_map/pallas_call | solution.py:365

commit v3 on v2

v3 whole, which is shorter than its diff:
```python
import functools
import math

import jax
import jax.numpy as jnp
from jax import lax
from jax.experimental import pallas as pl
from jax.experimental.pallas import tpu as pltpu
from jax.sharding import PartitionSpec as P

MESH = pl.DeviceIdType.MESH
F32 = jnp.float32
BF16 = jnp.bfloat16
LANES = 128
BLOCK = 256
FINE = 16
VMEM_LIMIT = 60 * 2**20
SPLIT = ((0, 8), (8, 16))
NT = (((1,), (1,)), ((), ()))


def cos_sin(steps, waves, count, inverse):
    product = steps * waves
    turns = jnp.floor(product * inverse + 0.5)
    half = (product - turns * count) * inverse * math.pi
    square = half * half
    sine = half
    term = 1.0
    series_s, series_c = 0.0, 0.0
    for power in range(5, -1, -1):
        series_s = series_s * square + (-1.0) ** power / math.factorial(2 * power + 1)
    for power in range(6, -1, -1):
        series_c = series_c * square + (-1.0) ** power / math.factorial(2 * power)
    sine = half * series_s
    return 1.0 - 2.0 * sine * sine, 2.0 * sine * series_c


def kernel(
    shape,
    grid_ref, counts_ref, weights_ref, waves_smem, wave_row, stiffness_ref, legendre_ref,
    out_ref,
    waves_ref, tables, turn_c, turn_s, small_c, small_s, flat, back, spread, basis, ordered, perm,
    damping, points, operand, turned, send_a, recv_a, send_b, recv_b, basis_sem, send_sems, recv_sems,
):
    holders, pairs, fields, length, slots, width = shape
    blocks = -(-length // BLOCK)
    me = lax.axis_index("lat")
    lev = lax.axis_index("lev")

    barrier = pltpu.get_barrier_semaphore()

    def greet(k, carry):
        other = lax.rem(me + k, holders)
        pl.semaphore_signal(barrier, inc=1, device_id=(other, lev), device_id_type=MESH)
        return carry

    lax.fori_loop(1, holders, greet, 0)
    load_basis = pltpu.make_async_copy(legendre_ref, basis, basis_sem)
    load_basis.start()

    for chunk, (_, count) in enumerate(SPLIT):
        held = pairs * slots * 4 * count
        rest = -held % (2 * LANES)
        if rest:
            flat[pl.ds(held, rest), :] = jnp.zeros((rest, LANES), F32)
            back[pl.ds(held, rest), :] = jnp.zeros((rest, LANES), F32)
        points[chunk][...] = jnp.zeros_like(points[chunk])

    for i in range(pairs):
        place = lax.broadcasted_iota(jnp.int32, (holders, width), 0) * pairs + i
        at = lax.broadcasted_iota(jnp.int32, (holders, width), 1)
        perm[i * holders : (i + 1) * holders, :] = jnp.where(at == place, 1.0, 0.0).astype(BF16)
    order = wave_row[...].reshape(1, width)
    first = lax.broadcasted_iota(jnp.int32, (16, width), 0) == 0
    digits = jnp.where(first, order // LANES, lax.rem(order, LANES))
    digits = lax.dot_general(
        digits.astype(F32).astype(BF16), perm[...], NT, preferred_element_type=F32
    )
    waves_ref[...] = digits[:1] * LANES + digits[1:2]

    def build_tables(i):
        count = jnp.full((1, width), counts_ref[i].astype(F32), F32)
        inverse = 1.0 / count
        waves = waves_ref[...]
        steps = lax.broadcasted_iota(jnp.int32, (FINE, width), 0).astype(F32)
        fine_c, fine_s = cos_sin(steps, waves, count, inverse)
        coarse_c, coarse_s = cos_sin(steps * FINE, waves, count, inverse)
        block_c, block_s = cos_sin(steps * BLOCK, waves, count, inverse)
        small_c[...] = coarse_c
        small_s[...] = coarse_s
        turn_c[i] = block_c
        turn_s[i] = block_s
        for g in range(BLOCK // FINE):
            c = small_c[g : g + 1, :]
            s = small_s[g : g + 1, :]
            tables[i, g * FINE : (g + 1) * FINE, :width] = (fine_c * c - fine_s * s).astype(BF16)
            tables[i, g * FINE : (g + 1) * FINE, width:] = (fine_s * c + fine_c * s).astype(BF16)

    def row_of(i, s, count, h, r):
        return pl.multiple_of(((i * slots + s) * 4 + h * 2 + r) * count, 8)

    def analyse(i, chunk):
        start, count = SPLIT[chunk]
        rows = 2 * count
        total = counts_ref[i]
        for t in range(blocks):
            size = min(BLOCK, length - t * BLOCK)
            at = lax.broadcasted_iota(jnp.int32, (rows, size), 1) + t * BLOCK
            values = grid_ref[i, :, start : start + count, t * BLOCK : t * BLOCK + size].astype(F32)
            values = jnp.where(at < total, values.reshape(rows, size), 0.0)
            points[chunk][t * rows : (t + 1) * rows, :size] = values.astype(BF16)
        limit = total.astype(F32)
        scale = jnp.full((1, BLOCK), weights_ref[i], F32) / jnp.full((1, BLOCK), limit, F32)
        for n in range(width // BLOCK):
            lanes = slice(n * BLOCK, (n + 1) * BLOCK)
            by_c = jnp.dot(points[chunk][...], tables[i, :, lanes], preferred_element_type=F32)
            by_s = jnp.dot(
                points[chunk][...],
                tables[i, :, width + n * BLOCK : width + (n + 1) * BLOCK],
                preferred_element_type=F32,
            )
            real = by_c[:rows]
            imag = by_s[:rows]
            for t in range(1, blocks):
                c = turn_c[i, t : t + 1, lanes]
                s = turn_s[i, t : t + 1, lanes]
                zc = by_c[t * rows : (t + 1) * rows]
                zs = by_s[t * rows : (t + 1) * rows]
                real = real + (c * zc - s * zs)
                imag = imag + (s * zc + c * zs)
            inside = 2.0 * waves_ref[:, lanes] < limit
            factor = jnp.where(inside, scale, 0.0)
            real = real * factor
            imag = -imag * factor
            for k in range(BLOCK // LANES):
                slot = n * (BLOCK // LANES) + k
                cut = slice(k * LANES, (k + 1) * LANES)
                for h in range(2):
                    part = slice(h * count, (h + 1) * count)
                    flat[pl.ds(row_of(i, slot, count, h, 0), count), :] = real[part, cut]
                    flat[pl.ds(row_of(i, slot, count, h, 1), count), :] = imag[part, cut]

    def pack(source, target):
        deep = 2 * target.shape[1]
        for q in range(deep):
            piece = source[q * LANES : (q + 1) * LANES, :]
            spread[pl.ds(q, holders, stride=deep), :] = piece.T
        twos = spread[pl.ds(0, holders * deep), :].reshape(holders * deep // 2, 2, LANES).astype(BF16)
        target[...] = twos.reshape(holders, deep // 2, 2, LANES)

    def unpack(source):
        deep = 2 * source.shape[1]
        spread[pl.ds(0, holders * deep), :] = source[...].astype(F32).reshape(holders * deep, LANES)
        for q in range(deep):
            flat[q * LANES : (q + 1) * LANES, :] = spread[pl.ds(q, holders, stride=deep), :].T

    def send(source, target, sem):
        def one(k, carry):
            other = lax.rem(me + k, holders)
            pltpu.make_async_remote_copy(
                src_ref=source.at[other],
                dst_ref=target.at[me],
                send_sem=send_sems.at[sem],
                recv_sem=recv_sems.at[sem],
                device_id=(other, lev),
                device_id_type=MESH,
            ).start()
            return carry

        lax.fori_loop(1, holders, one, 0)
        target[me] = source[me]

    def finish(ref, sem):
        most = ref.at[pl.ds(0, holders - 1)]
        pltpu.make_async_copy(most, most, sem).wait()

    chunks = len(SPLIT)
    for chunk in range(chunks):
        def step(i, carry):
            if chunk == 0:
                build_tables(i)
            analyse(i, chunk)
            return carry

        lax.fori_loop(0, pairs, step, 0)
        pack(flat, send_a[chunk])
        if chunk == 0:
            pl.semaphore_wait(barrier, holders - 1)
        send(send_a[chunk], recv_a[chunk], chunk)

    load_basis.wait()
    levels = lax.broadcasted_iota(jnp.int32, (fields, stiffness_ref.shape[1]), 0) + lev * fields
    column = lax.broadcasted_iota(jnp.int32, (fields, stiffness_ref.shape[1]), 1)
    stiffness = jnp.sum(jnp.where(levels == column, stiffness_ref[...], 0.0), axis=1, keepdims=True)
    offsets = lax.broadcasted_iota(jnp.int32, (1, width), 1)
    parity = (1 - 2 * lax.rem(offsets, 2)).astype(F32)

    def prepare(s, carry):
        for m in range(width // BLOCK):
            part = slice(m * BLOCK, (m + 1) * BLOCK)
            ordered[s, part, :] = jnp.dot(
                perm[part, :], basis[s], preferred_element_type=F32
            ).astype(BF16)
        wave = waves_smem[me * slots + s]
        degrees = (offsets + wave).astype(F32)
        factor = 1.0 / (1.0 + stiffness * degrees * (degrees + 1.0))
        damping[s] = jnp.where(offsets < width - wave, factor, 0.0)
        return carry

    lax.fori_loop(0, slots, prepare, 0)

    for chunk, (start, count) in enumerate(SPLIT):
        finish(recv_a[chunk], recv_sems.at[chunk])
        unpack(recv_a[chunk])

        def transform(s, carry):
            parts = [flat[pl.ds(row_of(i, s, count, 0, 0), 4 * count), :].astype(BF16) for i in range(pairs)]
            spectra = jnp.dot(
                jnp.concatenate(parts, axis=1), ordered[s], preferred_element_type=F32
            )
            combined = spectra[: 2 * count] + parity * spectra[2 * count :]
            damp = damping[s, start : start + count, :]
            scaled = combined * jnp.concatenate([damp, damp], axis=0)
            both = jnp.concatenate([scaled.astype(BF16), (scaled * parity).astype(BF16)], axis=0)
            result = lax.dot_general(both, ordered[s], NT, preferred_element_type=F32)
            for i in range(pairs):
                back[pl.ds(row_of(i, s, count, 0, 0), 4 * count), :] = result[
                    :, i * holders : (i + 1) * holders
                ]
            return carry

        lax.fori_loop(0, slots, transform, 0)
        pack(back, send_b[chunk])
        send(send_b[chunk], recv_b[chunk], chunks + chunk)

    def synthesise(i, chunk):
        start, count = SPLIT[chunk]
        rows = 2 * count
        total = counts_ref[i]
        inside = 2.0 * waves_ref[...] < total.astype(F32)
        weight = jnp.where(inside, jnp.where(waves_ref[...] == 0, 1.0, 2.0), 0.0)
        for s in range(slots):
            lanes = slice(s * LANES, (s + 1) * LANES)
            for h in range(2):
                part = slice(h * count, (h + 1) * count)
                for r in range(2):
                    operand[r, part, lanes] = (
                        flat[pl.ds(row_of(i, s, count, h, r), count), :] * weight[:, lanes]
                    )
        for n in range(width // BLOCK):
            lanes = slice(n * BLOCK, (n + 1) * BLOCK)
            real = operand[0, :rows, lanes]
            imag = operand[1, :rows, lanes]
            for t in range(blocks):
                c = turn_c[i, t : t + 1, lanes]
                s = turn_s[i, t : t + 1, lanes]
                turned[t * rows : (t + 1) * rows, lanes] = (real * c - imag * s).astype(BF16)
                turned[t * rows : (t + 1) * rows, width + n * BLOCK : width + (n + 1) * BLOCK] = (
                    -(real * s + imag * c)
                ).astype(BF16)
        result = lax.dot_general(
            turned[: blocks * rows, :], tables[i], NT, preferred_element_type=F32
        )
        for t in range(blocks):
            size = min(BLOCK, length - t * BLOCK)
            at = lax.broadcasted_iota(jnp.int32, (rows, size), 1) + t * BLOCK
            values = jnp.where(at < total, result[t * rows : (t + 1) * rows, :size], 0.0)
            out_ref[i, :, start : start + count, t * BLOCK : t * BLOCK + size] = values.reshape(
                2, count, size
            ).astype(BF16)

    for chunk in range(chunks):
        finish(recv_b[chunk], recv_sems.at[chunks + chunk])
        unpack(recv_b[chunk])

        def step_back(i, carry):
            synthesise(i, chunk)
            return carry

        lax.fori_loop(0, pairs, step_back, 0)

    for chunk in range(chunks):
        finish(send_a[chunk], send_sems.at[chunk])
        finish(send_b[chunk], send_sems.at[chunks + chunk])


def write_out(source, target, sems):
    copies = [
        pltpu.make_async_copy(source.at[i], target.at[i], sems.at[i])
        for i in range(source.shape[0])
    ]
    for copy in copies:
        copy.start()
    for copy in copies:
        copy.wait()


def solution(mesh):
    holders = mesh.shape["lat"]

    def on_device(grid, point_counts, waves, legendre, weights, stiffness):
        pairs, _, fields, length = grid.shape
        slots, latitudes, width = legendre.shape
        blocks = -(-length // BLOCK)
        most = max(count for _, count in SPLIT)
        deep = [-(-pairs * slots * 4 * count // (2 * LANES)) for _, count in SPLIT]
        messages = [pltpu.VMEM((holders, pieces, 2, LANES), BF16) for pieces in deep]
        assert pairs == slots and holders * slots == width == latitudes
        assert sum(count for _, count in SPLIT) == fields
        smem = pl.BlockSpec(memory_space=pltpu.SMEM)
        vmem = pl.BlockSpec(memory_space=pltpu.VMEM)
        result = pl.pallas_call(
            functools.partial(kernel, (holders, pairs, fields, length, slots, width)),
            out_shape=pltpu.VMEM(grid.shape, grid.dtype),
            in_specs=[vmem, smem, smem, smem, vmem, vmem, pl.BlockSpec(memory_space=pl.ANY)],
            out_specs=vmem,
            scratch_shapes=[
                pltpu.VMEM((1, width), F32),
                pltpu.VMEM((pairs, BLOCK, 2 * width), BF16),
                pltpu.VMEM((pairs, FINE, width), F32),
                pltpu.VMEM((pairs, FINE, width), F32),
                pltpu.VMEM((FINE, width), F32),
                pltpu.VMEM((FINE, width), F32),
                pltpu.VMEM((2 * max(deep) * LANES, LANES), F32),
                pltpu.VMEM((2 * max(deep) * LANES, LANES), F32),
                pltpu.VMEM((2 * max(deep) * holders, LANES), F32),
                pltpu.VMEM((slots, latitudes, width), BF16),
                pltpu.VMEM((slots, latitudes, width), BF16),
                pltpu.VMEM((latitudes, width), BF16),
                pltpu.VMEM((slots, fields, width), F32),
                [pltpu.VMEM((blocks * 2 * count, BLOCK), BF16) for _, count in SPLIT],
                pltpu.VMEM((2, 2 * most, width), F32),
                pltpu.VMEM((blocks * 2 * most, 2 * width), BF16),
                messages,
                messages,
                messages,
                messages,
                pltpu.SemaphoreType.DMA,
                pltpu.SemaphoreType.DMA((2 * len(SPLIT),)),
                pltpu.SemaphoreType.DMA((2 * len(SPLIT),)),
            ],
            compiler_params=pltpu.CompilerParams(
                collective_id=0, has_side_effects=True, vmem_limit_bytes=VMEM_LIMIT
            ),
        )(grid, point_counts, weights, waves, waves, stiffness.reshape(1, -1), legendre)
        anywhere = pl.BlockSpec(memory_space=pl.ANY)
        return pl.pallas_call(
            write_out,
            out_shape=jax.ShapeDtypeStruct(grid.shape, grid.dtype),
            in_specs=[vmem],
            out_specs=anywhere,
            scratch_shapes=[pltpu.SemaphoreType.DMA((pairs,))],
        )(pltpu.with_memory_space_constraint(result, pltpu.VMEM))

    in_specs = (P("lat", None, "lev", None), P("lat"), P(), P("lat", None, None), P("lat"), P())
    out_specs = P("lat", None, "lev", None)
    return jax.shard_map(
        on_device, mesh=mesh, in_specs=in_specs, out_specs=out_specs, check_vma=False
    )
```

time: 68.7 us -> 64.8 us (0.943)
  Pallas kernels: 68.5 us -> 64.7 us
    pallas_call x1, Pallas kernels: 67.3 us -> 63.4 us  [on_device(): pl.pallas_call(functools.partial(kernel, (holders, pairs, fields, length,...]
where the time goes in v3:
time: 64.8 us; the launch traced here: 64.7 us
  Pallas kernels  64.7 us (100%)
    pallas_call x1, Pallas kernels, on_device(): pl.pallas_call(functools.partial(kernel, (holders, pairs, fields, length,...  63.4 us

profile of v3, /device:TPU:6, one launch (start us, length us, event | category | flops | bytes accessed | tf_op | source)
XLA Modules:
  0.0 64.7 jit_solution(9326873852285760117)
XLA Ops:
  0.0 63.4 %shard_map.64.source = bf16[6,2,24,3088]{3,2,1,0:T(8,128)(2,1)S(1)} custom-call(bf16[6,2,24,3088]{3,2,1,0:T(8,128)(2,1)} %grid_ref.1, s32[6]{0:T(128)} %counts_ref.1, f32[6]{0:T(128)} %weights_ref.1, s32[768]{0:T(1024)} %wave_row.1, s32[768]{0:T(1024)} %wave_row.1, f32[1,48]{1,0:T(1,128)} %bitcast.1, bf16[6,768,768]{2,1,0:T(8,128)(2,1)} %legendre_ref.1), custom_call_target="tpu_custom_call" | custom-call | tf_op jit(solution)/shard_map/pallas_call | solution.py:312
  63.5 1.3 %shard_map.65 = bf16[6,2,24,3088]{3,2,1,0:T(8,128)(2,1)} custom-call(bf16[6,2,24,3088]{3,2,1,0:T(8,128)(2,1)S(1)} %shard_map.64.source), custom_call_target="tpu_custom_call" | custom-call | tf_op jit(solution)/shard_map/pallas_call | solution.py:347

commit v4 on v3

--- a/solution.py
+++ b/solution.py
@@ -16,6 +16,8 @@
 FINE = 16
 VMEM_LIMIT = 60 * 2**20
 SPLIT = ((0, 8), (8, 16))
+OUTWARD = (((0, 6),), ((0, 6),))
+HOMEWARD = (((0, 6),), ((0, 2), (2, 2), (4, 2)))
 NT = (((1,), (1,)), ((), ()))
 
 
@@ -40,6 +42,7 @@
     grid_ref, counts_ref, weights_ref, waves_smem, wave_row, stiffness_ref, legendre_ref,
     out_ref,
     waves_ref, tables, turn_c, turn_s, small_c, small_s, flat, back, spread, basis, ordered, perm,
+    scaled,
     damping, points, operand, turned, send_a, recv_a, send_b, recv_b, basis_sem, send_sems, recv_sems,
 ):
     holders, pairs, fields, length, slots, width = shape
@@ -58,13 +61,9 @@
     load_basis = pltpu.make_async_copy(legendre_ref, basis, basis_sem)
     load_basis.start()
 
-    for chunk, (_, count) in enumerate(SPLIT):
-        held = pairs * slots * 4 * count
-        rest = -held % (2 * LANES)
-        if rest:
-            flat[pl.ds(held, rest), :] = jnp.zeros((rest, LANES), F32)
-            back[pl.ds(held, rest), :] = jnp.zeros((rest, LANES), F32)
-        points[chunk][...] = jnp.zeros_like(points[chunk])
+    spread[...] = jnp.zeros_like(spread)
+    for ref in points:
+        ref[...] = jnp.zeros_like(ref)
 
     for i in range(pairs):
         place = lax.broadcasted_iota(jnp.int32, (holders, width), 0) * pairs + i
@@ -140,19 +139,27 @@
                     flat[pl.ds(row_of(i, slot, count, h, 0), count), :] = real[part, cut]
                     flat[pl.ds(row_of(i, slot, count, h, 1), count), :] = imag[part, cut]
 
-    def pack(source, target):
+    def cut_of(chunk, first, number):
+        size = slots * 4 * SPLIT[chunk][1]
+        return first * size, number * size // LANES
+
+    def pack(source, target, cut):
         deep = 2 * target.shape[1]
-        for q in range(deep):
-            piece = source[q * LANES : (q + 1) * LANES, :]
+        base, pieces = cut
+        for q in range(pieces):
+            piece = source[base + q * LANES : base + (q + 1) * LANES, :]
             spread[pl.ds(q, holders, stride=deep), :] = piece.T
         twos = spread[pl.ds(0, holders * deep), :].reshape(holders * deep // 2, 2, LANES).astype(BF16)
         target[...] = twos.reshape(holders, deep // 2, 2, LANES)
 
-    def unpack(source):
+    def unpack(source, cut):
         deep = 2 * source.shape[1]
+        base, pieces = cut
         spread[pl.ds(0, holders * deep), :] = source[...].astype(F32).reshape(holders * deep, LANES)
-        for q in range(deep):
-            flat[q * LANES : (q + 1) * LANES, :] = spread[pl.ds(q, holders, stride=deep), :].T
+        for q in range(pieces):
+            flat[base + q * LANES : base + (q + 1) * LANES, :] = spread[
+                pl.ds(q, holders, stride=deep), :
+            ].T
 
     def send(source, target, sem):
         def one(k, carry):
@@ -174,19 +181,20 @@
         most = ref.at[pl.ds(0, holders - 1)]
         pltpu.make_async_copy(most, most, sem).wait()
 
-    chunks = len(SPLIT)
-    for chunk in range(chunks):
+    outward = [(chunk, cut) for chunk, cuts in enumerate(OUTWARD) for cut in cuts]
+    homeward = [(chunk, cut) for chunk, cuts in enumerate(HOMEWARD) for cut in cuts]
+    for index, (chunk, (first_lat, number)) in enumerate(outward):
         def step(i, carry):
             if chunk == 0:
                 build_tables(i)
             analyse(i, chunk)
             return carry
 
-        lax.fori_loop(0, pairs, step, 0)
-        pack(flat, send_a[chunk])
-        if chunk == 0:
+        lax.fori_loop(first_lat, first_lat + number, step, 0)
+        pack(flat, send_a[index], cut_of(chunk, first_lat, number))
+        if index == 0:
             pl.semaphore_wait(barrier, holders - 1)
-        send(send_a[chunk], recv_a[chunk], chunk)
+        send(send_a[index], recv_a[index], index)
 
     load_basis.wait()
     levels = lax.broadcasted_iota(jnp.int32, (fields, stiffness_ref.shape[1]), 0) + lev * fields
@@ -210,28 +218,44 @@
     lax.fori_loop(0, slots, prepare, 0)
 
     for chunk, (start, count) in enumerate(SPLIT):
-        finish(recv_a[chunk], recv_sems.at[chunk])
-        unpack(recv_a[chunk])
-
-        def transform(s, carry):
+        for index, (of, cut) in enumerate(outward):
+            if of == chunk:
+                finish(recv_a[index], recv_sems.at[index])
+                unpack(recv_a[index], cut_of(chunk, *cut))
+
+        def project(s, carry):
             parts = [flat[pl.ds(row_of(i, s, count, 0, 0), 4 * count), :].astype(BF16) for i in range(pairs)]
             spectra = jnp.dot(
                 jnp.concatenate(parts, axis=1), ordered[s], preferred_element_type=F32
             )
             combined = spectra[: 2 * count] + parity * spectra[2 * count :]
             damp = damping[s, start : start + count, :]
-            scaled = combined * jnp.concatenate([damp, damp], axis=0)
-            both = jnp.concatenate([scaled.astype(BF16), (scaled * parity).astype(BF16)], axis=0)
-            result = lax.dot_general(both, ordered[s], NT, preferred_element_type=F32)
-            for i in range(pairs):
-                back[pl.ds(row_of(i, s, count, 0, 0), 4 * count), :] = result[
-                    :, i * holders : (i + 1) * holders
-                ]
+            north = combined * jnp.concatenate([damp, damp], axis=0)
+            scaled[s, : 2 * count, :] = north.astype(BF16)
+            scaled[s, 2 * count : 4 * count, :] = (north * parity).astype(BF16)
             return carry
 
-        lax.fori_loop(0, slots, transform, 0)
-        pack(back, send_b[chunk])
-        send(send_b[chunk], recv_b[chunk], chunks + chunk)
+        lax.fori_loop(0, slots, project, 0)
+        for index, (of, (first_lat, number)) in enumerate(homeward):
+            if of != chunk:
+                continue
+
+            def restore(s, carry):
+                result = lax.dot_general(
+                    scaled[s, : 4 * count, :],
+                    ordered[s, first_lat * holders : (first_lat + number) * holders, :],
+                    NT,
+                    preferred_element_type=F32,
+                )
+                for i in range(number):
+                    back[pl.ds(row_of(first_lat + i, s, count, 0, 0), 4 * count), :] = result[
+                        :, i * holders : (i + 1) * holders
+                    ]
+                return carry
+
+            lax.fori_loop(0, slots, restore, 0)
+            pack(back, send_b[index], cut_of(chunk, first_lat, number))
+            send(send_b[index], recv_b[index], len(outward) + index)
 
     def synthesise(i, chunk):
         start, count = SPLIT[chunk]
@@ -269,19 +293,20 @@
                 2, count, size
             ).astype(BF16)
 
-    for chunk in range(chunks):
-        finish(recv_b[chunk], recv_sems.at[chunks + chunk])
-        unpack(recv_b[chunk])
+    for index, (chunk, (first_lat, number)) in enumerate(homeward):
+        finish(recv_b[index], recv_sems.at[len(outward) + index])
+        unpack(recv_b[index], cut_of(chunk, first_lat, number))
 
         def step_back(i, carry):
             synthesise(i, chunk)
             return carry
 
-        lax.fori_loop(0, pairs, step_back, 0)
-
-    for chunk in range(chunks):
-        finish(send_a[chunk], send_sems.at[chunk])
-        finish(send_b[chunk], send_sems.at[chunks + chunk])
+        lax.fori_loop(first_lat, first_lat + number, step_back, 0)
+
+    for index in range(len(outward)):
+        finish(send_a[index], send_sems.at[index])
+    for index in range(len(homeward)):
+        finish(send_b[index], send_sems.at[len(outward) + index])
 
 
 def write_out(source, target, sems):
@@ -303,8 +328,18 @@
         slots, latitudes, width = legendre.shape
         blocks = -(-length // BLOCK)
         most = max(count for _, count in SPLIT)
-        deep = [-(-pairs * slots * 4 * count // (2 * LANES)) for _, count in SPLIT]
-        messages = [pltpu.VMEM((holders, pieces, 2, LANES), BF16) for pieces in deep]
+        def messages(plan):
+            sizes = [
+                number * slots * 4 * SPLIT[chunk][1]
+                for chunk, cuts in enumerate(plan)
+                for _, number in cuts
+            ]
+            assert all(size % LANES == 0 for size in sizes)
+            return [pltpu.VMEM((holders, -(-size // (2 * LANES)), 2, LANES), BF16) for size in sizes]
+
+        outward, homeward = messages(OUTWARD), messages(HOMEWARD)
+        deep = 2 * max(message.shape[1] for message in outward + homeward)
+        held = pairs * slots * 4 * most
         assert pairs == slots and holders * slots == width == latitudes
         assert sum(count for _, count in SPLIT) == fields
         smem = pl.BlockSpec(memory_space=pltpu.SMEM)
@@ -321,23 +356,24 @@
                 pltpu.VMEM((pairs, FINE, width), F32),
                 pltpu.VMEM((FINE, width), F32),
                 pltpu.VMEM((FINE, width), F32),
-                pltpu.VMEM((2 * max(deep) * LANES, LANES), F32),
-                pltpu.VMEM((2 * max(deep) * LANES, LANES), F32),
-                pltpu.VMEM((2 * max(deep) * holders, LANES), F32),
+                pltpu.VMEM((held, LANES), F32),
+                pltpu.VMEM((held, LANES), F32),
+                pltpu.VMEM((deep * holders, LANES), F32),
                 pltpu.VMEM((slots, latitudes, width), BF16),
                 pltpu.VMEM((slots, latitudes, width), BF16),
                 pltpu.VMEM((latitudes, width), BF16),
+                pltpu.VMEM((slots, 4 * most, width), BF16),
                 pltpu.VMEM((slots, fields, width), F32),
                 [pltpu.VMEM((blocks * 2 * count, BLOCK), BF16) for _, count in SPLIT],
                 pltpu.VMEM((2, 2 * most, width), F32),
                 pltpu.VMEM((blocks * 2 * most, 2 * width), BF16),
-                messages,
-                messages,
-                messages,
-                messages,
+                outward,
+                outward,
+                homeward,
+                homeward,
                 pltpu.SemaphoreType.DMA,
-                pltpu.SemaphoreType.DMA((2 * len(SPLIT),)),
-                pltpu.SemaphoreType.DMA((2 * len(SPLIT),)),
+                pltpu.SemaphoreType.DMA((len(outward) + len(homeward),)),
+                pltpu.SemaphoreType.DMA((len(outward) + len(homeward),)),
             ],
             compiler_params=pltpu.CompilerParams(
                 collective_id=0, has_side_effects=True, vmem_limit_bytes=VMEM_LIMIT

time: 64.8 us -> 62.2 us (0.960)
  Pallas kernels: 64.7 us -> 61.6 us
    pallas_call x1, Pallas kernels: 63.4 us -> 60.3 us  [on_device(): pl.pallas_call(functools.partial(kernel, (holders, pairs, fields, length,...]
where the time goes in v4:
time: 62.2 us; the launch traced here: 61.6 us
  Pallas kernels  61.6 us (99%)
    pallas_call x1, Pallas kernels, on_device(): pl.pallas_call(functools.partial(kernel, (holders, pairs, fields, length,...  60.3 us
    pallas_call x1, Pallas kernels, on_device(): pl.pallas_call(write_out, out_shape=jax.ShapeDtypeStruct(grid.shape, grid...  1.28 us

profile of v4, /device:TPU:6, one launch (start us, length us, event | category | flops | bytes accessed | tf_op | source)
XLA Modules:
  0.0 61.6 jit_solution(15443089712261010263)
XLA Ops:
  0.0 60.3 %shard_map.64.source = bf16[6,2,24,3088]{3,2,1,0:T(8,128)(2,1)S(1)} custom-call(bf16[6,2,24,3088]{3,2,1,0:T(8,128)(2,1)} %grid_ref.1, s32[6]{0:T(128)} %counts_ref.1, f32[6]{0:T(128)} %weights_ref.1, s32[768]{0:T(1024)} %wave_row.1, s32[768]{0:T(1024)} %wave_row.1, f32[1,48]{1,0:T(1,128)} %bitcast.1, bf16[6,768,768]{2,1,0:T(8,128)(2,1)} %legendre_ref.1), custom_call_target="tpu_custom_call" | custom-call | tf_op jit(solution)/shard_map/pallas_call | solution.py:347
  60.4 1.3 %shard_map.65 = bf16[6,2,24,3088]{3,2,1,0:T(8,128)(2,1)} custom-call(bf16[6,2,24,3088]{3,2,1,0:T(8,128)(2,1)S(1)} %shard_map.64.source), custom_call_target="tpu_custom_call" | custom-call | tf_op jit(solution)/shard_map/pallas_call | solution.py:383

commit v5 on v4

--- a/solution.py
+++ b/solution.py
@@ -257,7 +257,7 @@
             pack(back, send_b[index], cut_of(chunk, first_lat, number))
             send(send_b[index], recv_b[index], len(outward) + index)
 
-    def synthesise(i, chunk):
+    def synthesise(i, chunk, room):
         start, count = SPLIT[chunk]
         rows = 2 * count
         total = counts_ref[i]
@@ -268,22 +268,22 @@
             for h in range(2):
                 part = slice(h * count, (h + 1) * count)
                 for r in range(2):
-                    operand[r, part, lanes] = (
+                    operand[room, r, part, lanes] = (
                         flat[pl.ds(row_of(i, s, count, h, r), count), :] * weight[:, lanes]
                     )
         for n in range(width // BLOCK):
             lanes = slice(n * BLOCK, (n + 1) * BLOCK)
-            real = operand[0, :rows, lanes]
-            imag = operand[1, :rows, lanes]
+            real = operand[room, 0, :rows, lanes]
+            imag = operand[room, 1, :rows, lanes]
             for t in range(blocks):
                 c = turn_c[i, t : t + 1, lanes]
                 s = turn_s[i, t : t + 1, lanes]
-                turned[t * rows : (t + 1) * rows, lanes] = (real * c - imag * s).astype(BF16)
-                turned[t * rows : (t + 1) * rows, width + n * BLOCK : width + (n + 1) * BLOCK] = (
+                turned[room, t * rows : (t + 1) * rows, lanes] = (real * c - imag * s).astype(BF16)
+                turned[room, t * rows : (t + 1) * rows, width + n * BLOCK : width + (n + 1) * BLOCK] = (
                     -(real * s + imag * c)
                 ).astype(BF16)
         result = lax.dot_general(
-            turned[: blocks * rows, :], tables[i], NT, preferred_element_type=F32
+            turned[room, : blocks * rows, :], tables[i], NT, preferred_element_type=F32
         )
         for t in range(blocks):
             size = min(BLOCK, length - t * BLOCK)
@@ -297,11 +297,13 @@
         finish(recv_b[index], recv_sems.at[len(outward) + index])
         unpack(recv_b[index], cut_of(chunk, first_lat, number))
 
-        def step_back(i, carry):
-            synthesise(i, chunk)
+        def step_back(n, carry):
+            synthesise(first_lat + 2 * n, chunk, 0)
+            synthesise(first_lat + 2 * n + 1, chunk, 1)
             return carry
 
-        lax.fori_loop(first_lat, first_lat + number, step_back, 0)
+        assert number % 2 == 0
+        lax.fori_loop(0, number // 2, step_back, 0)
 
     for index in range(len(outward)):
         finish(send_a[index], send_sems.at[index])
@@ -365,8 +367,8 @@
                 pltpu.VMEM((slots, 4 * most, width), BF16),
                 pltpu.VMEM((slots, fields, width), F32),
                 [pltpu.VMEM((blocks * 2 * count, BLOCK), BF16) for _, count in SPLIT],
-                pltpu.VMEM((2, 2 * most, width), F32),
-                pltpu.VMEM((blocks * 2 * most, 2 * width), BF16),
+                pltpu.VMEM((2, 2, 2 * most, width), F32),
+                pltpu.VMEM((2, blocks * 2 * most, 2 * width), BF16),
                 outward,
                 outward,
                 homeward,

time: 62.2 us -> 62 us (level)
  no operation moved by 1% of the time
where the time goes in v5:
time: 62 us; the launch traced here: 61.3 us
  Pallas kernels  61.3 us (99%)
    pallas_call x1, Pallas kernels, on_device(): pl.pallas_call(functools.partial(kernel, (holders, pairs, fields, length,...  60.1 us
    pallas_call x1, Pallas kernels, on_device(): pl.pallas_call(write_out, out_shape=jax.ShapeDtypeStruct(grid.shape, grid...  1.28 us

profile of v5, /device:TPU:6, one launch (start us, length us, event | category | flops | bytes accessed | tf_op | source)
XLA Modules:
  0.0 61.3 jit_solution(1451888164950931210)
XLA Ops:
  0.0 60.1 %shard_map.64.source = bf16[6,2,24,3088]{3,2,1,0:T(8,128)(2,1)S(1)} custom-call(bf16[6,2,24,3088]{3,2,1,0:T(8,128)(2,1)} %grid_ref.1, s32[6]{0:T(128)} %counts_ref.1, f32[6]{0:T(128)} %weights_ref.1, s32[768]{0:T(1024)} %wave_row.1, s32[768]{0:T(1024)} %wave_row.1, f32[1,48]{1,0:T(1,128)} %bitcast.1, bf16[6,768,768]{2,1,0:T(8,128)(2,1)} %legendre_ref.1), custom_call_target="tpu_custom_call" | custom-call | tf_op jit(solution)/shard_map/pallas_call | solution.py:349
  60.1 1.3 %shard_map.65 = bf16[6,2,24,3088]{3,2,1,0:T(8,128)(2,1)} custom-call(bf16[6,2,24,3088]{3,2,1,0:T(8,128)(2,1)S(1)} %shard_map.64.source), custom_call_target="tpu_custom_call" | custom-call | tf_op jit(solution)/shard_map/pallas_call | solution.py:385
